TPU v7x, 32 devices: a whole 2x2x4 slice. The times are simulated.
32 devices in a mesh: ctx: 8 (over y, x, core), mp: 4 (over z).
Axes of the slice: x: 2, y: 2, z: 4, core: 2. Of those that a mesh axis runs over, the one named last changes fastest.
Arguments:
- queries: bfloat16 [2048, 8192], P('ctx', 'mp'), may hold values from -6 to 6
- key_feats: bfloat16 [2048, 8192], P('ctx', 'mp'), may hold values from -6 to 6
- value_feats: bfloat16 [2048, 8192], P('ctx', 'mp'), may hold values from -6 to 6
- filters: bfloat16 [512, 128], P('mp'), may hold values from -0.5 to 0.5
- grad_out: bfloat16 [2048, 8192], P('ctx', 'mp'), may hold values from -40 to 40
Outputs:
- mixer_out: bfloat16 [2048, 8192], P('ctx', 'mp')
- grad_queries: bfloat16 [2048, 8192], P('ctx', 'mp')
- grad_keys: bfloat16 [2048, 8192], P('ctx', 'mp')
- grad_values: bfloat16 [2048, 8192], P('ctx', 'mp')
- grad_filters: float32 [512, 128], P('mp')
All inputs are finite; a program needn't handle non-finite values.
Results may differ from a plain program's by a relative error of at most 0.0058.
Values may be sent and summed in bfloat16 or wider, within the bound.
A program may use at most 64 MiB of HBM per device.

v0:
```python
import jax
import jax.numpy as jnp
from jax import lax
from jax.sharding import PartitionSpec as P

D = 8192
G = 16


def contract(formula, first_op, second_op):
    return jnp.einsum(formula, first_op, second_op, preferred_element_type=jnp.float32)


def toeplitz(filt):
    count, filter_len = filt.shape
    flipped = filt[:, ::-1]
    lead_zero = jnp.zeros((count, 1), filt.dtype)
    trailing = jnp.zeros((count, filter_len), filt.dtype)
    pattern = jnp.concatenate([lead_zero, flipped, trailing], axis=1)
    repeated = jnp.tile(pattern, (1, filter_len))
    return repeated[:, : filter_len * 2 * filter_len].reshape(count, filter_len, 2 * filter_len)


def make_windows(blocks, before):
    earlier = jnp.concatenate([before[:, :, None, :], blocks[:, :, :-1, :]], axis=2)
    return jnp.concatenate([earlier, blocks], axis=3)


def forward_conv(signal, before, toeplitz_mat):
    groups_here, group_size, seq_len = signal.shape
    filter_len = toeplitz_mat.shape[1]
    blocks = signal.reshape(groups_here, group_size, seq_len // filter_len, filter_len)
    window_rows = make_windows(blocks, before)
    result = contract("gam,gsnm->gsna", toeplitz_mat, window_rows)
    return (result.reshape(groups_here, group_size, seq_len), window_rows)


def backward_conv(grad_rows, after, toeplitz_mat):
    groups_here, group_size, seq_len = grad_rows.shape
    filter_len = toeplitz_mat.shape[1]
    blocks = grad_rows.reshape(groups_here, group_size, seq_len // filter_len, filter_len)
    spread = contract("gam,gsna->gsnm", toeplitz_mat, blocks)
    tail_part = contract("gam,gsa->gsm", toeplitz_mat, after)
    next_part = jnp.concatenate(
        [spread[:, :, 1:, :filter_len], tail_part[:, :, None, :filter_len]], axis=2
    )
    return (spread[:, :, :, filter_len:] + next_part).reshape(groups_here, group_size, seq_len)


def filter_grad(grad_rows, window_rows, filter_len):
    groups_here, group_size, seq_len = grad_rows.shape
    blocks = grad_rows.reshape(groups_here, group_size, seq_len // filter_len, filter_len)
    correlate = contract("gsna,gsnm->gam", blocks, window_rows)
    flattened = correlate.reshape(groups_here, filter_len * 2 * filter_len)
    flattened = jnp.concatenate(
        [flattened, jnp.zeros((groups_here, filter_len), jnp.float32)], axis=1
    )
    flattened = flattened.reshape(groups_here, filter_len, 2 * filter_len + 1)
    diagonals = jnp.sum(flattened, axis=1)
    return diagonals[:, 1 : filter_len + 1][:, ::-1]


def shards(queries, key_feats, value_feats, filters, grad_out):
    tokens, channels = queries.shape
    slab_groups, filter_len = filters.shape
    product = (
        (key_feats.astype(jnp.float32) * value_feats.astype(jnp.float32)).astype(jnp.bfloat16).T
    )
    grad_mix = (grad_out.astype(jnp.float32) * queries.astype(jnp.float32)).astype(jnp.bfloat16).T
    owners = lax.axis_size("ctx")
    own_width = channels // owners
    own_groups = own_width // G
    signal = lax.all_to_all(product, "ctx", split_axis=0, concat_axis=1, tiled=True)
    grad_rows = lax.all_to_all(grad_mix, "ctx", split_axis=0, concat_axis=1, tiled=True)
    seq_len = signal.shape[1]
    signal = signal.reshape(own_groups, G, seq_len)
    grad_rows = grad_rows.reshape(own_groups, G, seq_len)
    first_group = lax.axis_index("ctx") * own_groups
    own_filters = lax.dynamic_slice_in_dim(filters, first_group, own_groups, 0)
    toeplitz_mat = toeplitz(own_filters)
    zero_rim = jnp.zeros((own_groups, G, filter_len), jnp.bfloat16)
    conv_out, window_rows = forward_conv(signal, zero_rim, toeplitz_mat)
    conv_out = conv_out.astype(jnp.bfloat16).reshape(own_width, seq_len)
    conv_grad = (
        backward_conv(grad_rows, zero_rim, toeplitz_mat)
        .astype(jnp.bfloat16)
        .reshape(own_width, seq_len)
    )
    partial_grad = filter_grad(grad_rows, window_rows, filter_len)
    conv_rows = lax.all_to_all(conv_out, "ctx", split_axis=1, concat_axis=0, tiled=True)
    grad_back = lax.all_to_all(conv_grad, "ctx", split_axis=1, concat_axis=0, tiled=True)
    raw_filters = lax.all_gather(partial_grad, "ctx", axis=0, tiled=True)
    conv_f = conv_rows.T.astype(jnp.float32)
    back_f = grad_back.T.astype(jnp.float32)
    mixer_out = (queries.astype(jnp.float32) * conv_f).astype(jnp.bfloat16)
    grad_queries = (grad_out.astype(jnp.float32) * conv_f).astype(jnp.bfloat16)
    grad_keys = (back_f * value_feats.astype(jnp.float32)).astype(jnp.bfloat16)
    grad_values = (back_f * key_feats.astype(jnp.float32)).astype(jnp.bfloat16)
    square_sum = lax.psum(jnp.sum(raw_filters * raw_filters), "mp")
    grad_rms = jnp.sqrt(square_sum / (D // G * filter_len) + 1e-06)
    grad_filters = raw_filters * jnp.minimum(1.0, 1.0 / grad_rms)
    return (mixer_out, grad_queries, grad_keys, grad_values, grad_filters)


def solution(mesh):
    placed = (P("ctx", "mp"), P("ctx", "mp"), P("ctx", "mp"), P("mp", None), P("ctx", "mp"))
    return jax.shard_map(
        shards,
        mesh=mesh,
        in_specs=placed,
        out_specs=(P("ctx", "mp"), P("ctx", "mp"), P("ctx", "mp"), P("ctx", "mp"), P("mp", None)),
        check_vma=False,
    )
```

profile of v0, /device:TPU:0, one launch (start us, length us, event | category | flops | bytes accessed | tf_op | source)
XLA Modules:
  0.0 122.7 jit_solution(6575762246150268738)
XLA Ops:
  0.6 1.9 %fusion.9 = bf16[2048,256]{0,1:T(8,128)(2,1)S(1)} fusion(bf16[256,2048]{1,0:T(8,128)(2,1)} %param.5, bf16[256,2048]{1,0:T(8,128)(2,1)} %param.9), kind=kLoop, calls=%fused_computation.18 | loop fusion | flops 2097152 | bytes 3145728 | tf_op jit(solution)/shard_map/transpose | solution.py:69
  2.6 1.3 %copy.26 = bf16[2048,256]{1,0:T(8,128)(2,1)} copy(bf16[2048,256]{0,1:T(8,128)(2,1)S(1)} %fusion.9) | data formatting | bytes 2097152 | tf_op jit(solution)/shard_map/transpose | solution.py:69
  3.9 5.2 %all-to-all-start.2 = ((bf16[8,256,256]{2,1,0:T(8,128)(2,1)}), bf16[8,256,256]{2,1,0:T(8,128)(2,1)}, u32[]{:S(2)}, u32[]{:S(2)}) async-start(bf16[8,256,256]{2,1,0:T(8,128)(2,1)} %bitcast.8), calls=%async_computation.2 | async-start | bytes 2097152 | tf_op jit(solution)/shard_map/all_to_all | solution.py:74
  9.5 1.8 %tile.10 = bf16[16,32896]{1,0:T(8,128)(2,1)S(1)} reshape(bf16[16,128,257]{2,1,0:T(8,128)(2,1)S(1)} %tile.4) | data formatting | bytes 2105344 | tf_op jit(solution)/shard_map/tile | solution.py:20
  11.9 12.7 %all-to-all-done.2 = bf16[8,256,256]{2,1,0:T(8,128)(2,1)} async-done(((bf16[8,256,256]{2,1,0:T(8,128)(2,1)}), bf16[8,256,256]{2,1,0:T(8,128)(2,1)}, u32[]{:S(2)}, u32[]{:S(2)}) %all-to-all-start.2) | async-done | bytes 1048608 | tf_op jit(solution)/shard_map/all_to_all | solution.py:74
  24.6 1.8 %copy.27 = bf16[256,8,256]{2,1,0:T(8,128)(2,1)S(1)} copy(bf16[256,8,256]{2,0,1:T(8,128)(2,1)} %bitcast.9) | data formatting | bytes 2097152 | tf_op jit(solution)/shard_map/all_to_all | solution.py:74
  26.4 0.4 reshape_reshape.8
  26.8 0.7 fusion.11
  28.1 0.4 fusion.8
  28.5 0.4 convert_element_type.89
  29.1 17.8 %all_to_all.52 = bf16[256,8,256]{2,0,1:T(8,128)(2,1)S(1)} all-to-all(bf16[256,8,256]{2,0,1:T(8,128)(2,1)S(1)} %copy.28), channel_id=1, replica_groups=mesh['ctx'=8,'mp'=4] {'ctx'}, dimensions={1} | all-to-all | bytes 2097152 | tf_op jit(solution)/shard_map/all_to_all | solution.py:91
  46.9 1.5 %convert_element_type.101 = f32[256,8,256]{2,0,1:T(8,128)} convert(bf16[256,8,256]{2,0,1:T(8,128)(2,1)S(1)} %all_to_all.52) | non-fusion elementwise | flops 524288 | bytes 3145728 | tf_op jit(solution)/shard_map/convert_element_type | solution.py:94
  48.4 1.9 %copy.29 = f32[2048,256]{0,1:T(8,128)S(1)} copy(f32[2048,256]{1,0:T(8,128)} %bitcast.44) | data formatting | bytes 4194304 | tf_op jit(solution)/shard_map/convert_element_type | solution.py:94
  50.4 4.0 %fusion.2 = (bf16[256,2048]{1,0:T(8,128)(2,1)}, bf16[256,2048]{1,0:T(8,128)(2,1)}, bf16[2048,256]{0,1:T(8,128)(2,1)}) fusion(bf16[256,2048]{1,0:T(8,128)(2,1)} %param.6, f32[2048,256]{0,1:T(8,128)S(1)} %copy.29, bf16[256,2048]{1,0:T(8,128)(2,1)} %param.7), kind=kLoop, calls=%fused_computation.9 | loop fusion | flops 4194304 | bytes 7340032 | tf_op jit(solution)/shard_map/convert_element_type | solution.py:98
  54.3 1.5 %copy.22 = bf16[2048,256]{1,0:T(8,128)(2,1)S(1)} copy(bf16[2048,256]{0,1:T(8,128)(2,1)} %get-tuple-element.7) | data formatting | bytes 2097152 | tf_op jit(solution)/shard_map/transpose | solution.py:67
  55.8 17.8 %all_to_all.53 = bf16[8,256,256]{2,1,0:T(8,128)(2,1)S(1)} all-to-all(bf16[8,256,256]{2,1,0:T(8,128)(2,1)S(1)} %bitcast.51), channel_id=1, replica_groups=mesh['ctx'=8,'mp'=4] {'ctx'}, dimensions={0} | all-to-all | bytes 2097152 | tf_op jit(solution)/shard_map/all_to_all | solution.py:73
  73.6 0.6 copy.23
  74.2 0.4 reshape_reshape.7
  74.6 0.7 convolution_convert_fusion
  75.7 1.2 copy.24
  76.9 4.4 %all-to-all-start.1 = ((bf16[256,8,256]{2,0,1:T(8,128)(2,1)}), bf16[256,8,256]{2,0,1:T(8,128)(2,1)}, u32[]{:S(2)}, u32[]{:S(2)}) async-start(bf16[256,8,256]{2,0,1:T(8,128)(2,1)} %copy.24), calls=%async_computation.1 | async-start | bytes 2097152 | tf_op jit(solution)/shard_map/all_to_all | solution.py:90
  81.3 0.6 fusion.14
  81.9 1.2 copy.34
  83.2 1.5 %concatenate.19 = f32[16,32896]{1,0:T(8,128)} pad(f32[16,32768]{1,0:T(8,128)S(1)} %bitcast.45, f32[]{:T(128)} %constant.5.clone.1), padding=0_0x0_128 | pad | bytes 4202500 | tf_op jit(solution)/shard_map/concatenate | solution.py:55
  84.6 3.7 %reshape.53 = f32[16,128,257]{2,1,0:T(8,128)S(1)} reshape(f32[16,32896]{1,0:T(8,128)} %concatenate.19) | data formatting | bytes 4210688 | tf_op jit(solution)/shard_map/reshape | solution.py:58
  88.7 11.1 %all_gather.3 = f32[128,128]{1,0:T(8,128)S(1)} all-gather(f32[16,128]{1,0:T(8,128)S(1)} %rev.7), channel_id=1, replica_groups=mesh['ctx'=8,'mp'=4] {'ctx'}, dimensions={0}, use_global_device_ids=true | all-gather | bytes 73728 | tf_op jit(solution)/shard_map/all_gather | solution.py:92
  99.9 0.6 multiply_reduce_fusion
  100.5 13.0 %psum.7 = f32[]{:T(128)} all-reduce(f32[]{:T(128)} %multiply_reduce_fusion), channel_id=1, replica_groups=mesh['ctx'=8,'mp'=4] {'mp'}, use_global_device_ids=true, to_apply=%region_2.0 | all-reduce | flops 1 | bytes 8 | tf_op jit(solution)/shard_map/psum | solution.py:99
  114.1 0.6 broadcast_multiply_fusion
  114.8 2.8 %convert_element_type.100 = f32[256,8,256]{2,0,1:T(8,128)} convert(bf16[256,8,256]{2,0,1:T(8,128)(2,1)} %all-to-all-done.1) | non-fusion elementwise | flops 524288 | bytes 3145728 | tf_op jit(solution)/shard_map/convert_element_type | solution.py:93
  117.5 2.0 %copy.25 = f32[2048,256]{0,1:T(8,128)S(1)} copy(f32[2048,256]{1,0:T(8,128)} %bitcast.46) | data formatting | bytes 4194304 | tf_op jit(solution)/shard_map/convert_element_type | solution.py:93
  119.6 3.1 %fusion.5 = (bf16[256,2048]{1,0:T(8,128)(2,1)}, bf16[256,2048]{1,0:T(8,128)(2,1)}) fusion(bf16[256,2048]{1,0:T(8,128)(2,1)S(1)} %copy-done.1, f32[2048,256]{0,1:T(8,128)S(1)} %copy.25, bf16[256,2048]{1,0:T(8,128)(2,1)} %param.5), kind=kLoop, calls=%fused_computation.12 | loop fusion | flops 3145728 | bytes 6291456 | tf_op jit(solution)/shard_map/convert_element_type | solution.py:96
  (25 shorter events, 2.5 us)
Async XLA Ops:
  0.6 8.5 %copy-start = (bf16[128,128]{1,0:T(8,128)(2,1)S(1)}, bf16[128,128]{1,0:T(8,128)(2,1)}, u32[]{:S(2)}) copy-start(bf16[128,128]{1,0:T(8,128)(2,1)} %param.8) | copy-start | bytes 98308
  3.9 20.7 %all-to-all-start.2 = ((bf16[8,256,256]{2,1,0:T(8,128)(2,1)}), bf16[8,256,256]{2,1,0:T(8,128)(2,1)}, u32[]{:S(2)}, u32[]{:S(2)}) async-start(bf16[8,256,256]{2,1,0:T(8,128)(2,1)} %bitcast.8), calls=%async_computation.2 | async-start | bytes 2097152 | tf_op jit(solution)/shard_map/all_to_all | solution.py:74
  26.8 1.0 copy-start.2
  75.7 5.6 %copy-start.3 = (bf16[16,16,16,128]{3,2,1,0:T(8,128)(2,1)S(1)}, bf16[16,16,16,128]{3,2,1,0:T(8,128)(2,1)}, u32[]{:S(2)}) copy-start(bf16[16,16,16,128]{3,2,1,0:T(8,128)(2,1)} %copy-done.2) | copy-start | bytes 3145732
  76.9 37.9 %all-to-all-start.1 = ((bf16[256,8,256]{2,0,1:T(8,128)(2,1)}), bf16[256,8,256]{2,0,1:T(8,128)(2,1)}, u32[]{:S(2)}, u32[]{:S(2)}) async-start(bf16[256,8,256]{2,0,1:T(8,128)(2,1)} %copy.24), calls=%async_computation.1 | async-start | bytes 2097152 | tf_op jit(solution)/shard_map/all_to_all | solution.py:90
  117.5 2.0 %copy-start.1 = (bf16[256,2048]{1,0:T(8,128)(2,1)S(1)}, bf16[256,2048]{1,0:T(8,128)(2,1)}, u32[]{:S(2)}) copy-start(bf16[256,2048]{1,0:T(8,128)(2,1)} %param.9) | copy-start | bytes 3145732
where the time goes:
time: 123 us
  blocking collectives  59.7 us (49%)
  local copies, waits for them, and re-layouts  21.6 us (18%)
  other arithmetic  15.3 us (12%)
  waiting for transfers between devices  12.7 us (10%)
  starting transfers between devices  9.58 us (8%)
  matrix products  2.25 us (2%)
  between operations  1.55 us (1%)
    all_to_all x1, blocking collectives, shards(): lax.all_to_all(conv_grad, 'ctx', split_axis=1, concat_axis=0, tiled=True)  17.8 us
    all_to_all x1, blocking collectives, shards(): lax.all_to_all(product, 'ctx', split_axis=0, concat_axis=1, tiled=True)  17.8 us
    psum x1, blocking collectives, shards(): square_sum = lax.psum(jnp.sum(raw_filters * raw_filters), 'mp')  13 us
    all_to_all x1, waiting for transfers between devices, shards(): lax.all_to_all(grad_mix, 'ctx', split_axis=0, concat_axis=1, tiled=True)  12.7 us
    all_gather x1, blocking collectives, shards(): raw_filters = lax.all_gather(partial_grad, 'ctx', axis=0, tiled=True)  11.1 us
    all_to_all x1, starting transfers between devices, shards(): lax.all_to_all(grad_mix, 'ctx', split_axis=0, concat_axis=1, tiled=True)  5.17 us
    all_to_all x1, starting transfers between devices, shards(): lax.all_to_all(conv_out, 'ctx', split_axis=1, concat_axis=0, tiled=True)  4.41 us
    convert_element_type x1, other arithmetic, shards(): grad_values = (back_f * key_feats.astype(jnp.float32)).astype(jnp.bfloat16)  3.98 us
  transfers between devices with their start and end apart: 2, of which 1 were waited for; matrix products, arithmetic and copies ran while one was open for 9% of the time, Pallas kernels for 0%

commit v1 on v0

v1 whole, which is shorter than its diff:
```python
import functools

import jax
import jax.numpy as jnp
from jax import lax
from jax.experimental import pallas as pl
from jax.experimental.pallas import tpu as pltpu
from jax.sharding import PartitionSpec as P

G = 16
MESH = pl.DeviceIdType.MESH
F32 = jnp.float32
BF16 = jnp.bfloat16
WIDE = 128
PARTS = 4


def times(a, b):
    return (a.astype(F32) * b.astype(F32)).astype(BF16)


def rows_dot(a, b):
    return lax.dot_general(a, b, (((1,), (1,)), ((), ())), preferred_element_type=F32)


def kernel(n_ctx, n_mp, q_ref, k_ref, v_ref, f_ref, g_ref,
           mix_ref, gq_ref, gk_ref, gv_ref, gf_ref,
           prod, gmix, phalo, ghalo, taps, toep, pt, gt, folded,
           partial, arrived, reduced, gathered, own_sq, all_sq,
           p_send, p_recv, g_send, g_recv,
           rs_send, rs_recv, ag_send, ag_recv, sq_send, sq_recv):
    tokens, channels = q_ref.shape
    groups, span = f_ref.shape
    blocks = tokens // span
    own = groups // n_ctx
    part = channels // PARTS
    me = lax.axis_index("ctx")
    slab = lax.axis_index("mp")
    per_chunk = WIDE // G

    def ctx_peer(i):
        return lax.rem(me + i, n_ctx)

    def mp_peer(i):
        return lax.rem(slab + i, n_mp)

    barrier = pltpu.get_barrier_semaphore()

    @pl.loop(1, n_ctx)
    def _(i):
        pl.semaphore_signal(barrier, inc=1, device_id=(ctx_peer(i), slab), device_id_type=MESH)

    @pl.loop(1, n_mp)
    def _(i):
        pl.semaphore_signal(barrier, inc=1, device_id=(me, mp_peer(i)), device_id_type=MESH)

    head, tail = slice(0, span), slice(tokens - span, tokens)
    gmix[head, :] = times(g_ref[head, :], q_ref[head, :])
    prod[tail, :] = times(k_ref[tail, :], v_ref[tail, :])
    pl.semaphore_wait(barrier, n_ctx + n_mp - 2)

    def g_copy(i):
        cols = slice(i * part, (i + 1) * part)
        return pltpu.make_async_remote_copy(
            src_ref=gmix.at[head, cols], dst_ref=ghalo.at[:, cols],
            send_sem=g_send.at[i], recv_sem=g_recv.at[i],
            device_id=(lax.rem(me + n_ctx - 1, n_ctx), slab), device_id_type=MESH)

    def p_copy(i):
        cols = slice(i * part, (i + 1) * part)
        return pltpu.make_async_remote_copy(
            src_ref=prod.at[tail, cols], dst_ref=phalo.at[:, cols],
            send_sem=p_send.at[i], recv_sem=p_recv.at[i],
            device_id=(lax.rem(me + 1, n_ctx), slab), device_id_type=MESH)

    for i in range(PARTS):
        @pl.when(me > 0)
        def _():
            g_copy(i).start()

        @pl.when(me < n_ctx - 1)
        def _():
            p_copy(i).start()

    @pl.when(me == 0)
    def _():
        phalo[...] = jnp.zeros_like(phalo)

    @pl.when(me == n_ctx - 1)
    def _():
        ghalo[...] = jnp.zeros_like(ghalo)

    rest_g, rest_p = slice(span, tokens), slice(0, tokens - span)
    gmix[rest_g, :] = times(g_ref[rest_g, :], q_ref[rest_g, :])
    prod[rest_p, :] = times(k_ref[rest_p, :], v_ref[rest_p, :])
    taps[...] = f_ref[...].astype(F32)

    col = lax.broadcasted_iota(jnp.int32, (span, span), 1)
    row = lax.broadcasted_iota(jnp.int32, (span, span), 0)
    upper = col >= row

    @pl.loop(0, groups)
    def _(i):
        line = jnp.broadcast_to(taps[pl.ds(i, 1), :], (span, span))
        turned = pltpu.roll(line, 0, 1, stride=1, stride_axis=0)
        zero = jnp.zeros_like(turned)
        toep[i, :, 0:span] = jnp.where(upper, turned, zero).astype(BF16)
        toep[i, :, span:] = jnp.where(upper, zero, turned).astype(BF16)

    @pl.loop(0, channels // WIDE)
    def _(c):
        at = pl.ds(pl.multiple_of(c * WIDE, WIDE), WIDE)
        pt[at, span:] = prod[:, at].T
        gt[at, 0:tokens] = gmix[:, at].T

    @pl.when(me < n_ctx - 1)
    def _():
        for i in range(PARTS):
            g_copy(i).wait_recv()

    @pl.loop(0, channels // WIDE)
    def _(c):
        at = pl.ds(pl.multiple_of(c * WIDE, WIDE), WIDE)
        gt[at, tokens:] = ghalo[:, at].T

    def windows(ref, at):
        x = ref[at, :]
        return jnp.concatenate(
            [x[:, n * span:(n + 2) * span] for n in range(blocks)], axis=0)

    @pl.loop(0, groups)
    def _(i):
        at = pl.ds(pl.multiple_of(i * G, G), G)
        x = pt[at, :]
        left = jnp.concatenate(
            [x[:, (n + 1) * span:(n + 2) * span] for n in range(blocks)], axis=0)
        both = lax.dot_general(left, windows(gt, at), (((0,), (0,)), ((), ())),
                               preferred_element_type=F32)
        turn = jnp.where(upper, both[:, :span], both[:, span:])
        half = span // 2
        while half >= 8:
            turn = turn[:half] + pltpu.roll(turn[half:], span - half, 1)
            half //= 2
        folded[pl.ds(pl.multiple_of(i * 8, 8), 8), :] = turn

    total = folded[pl.ds(0, groups, stride=8), :]
    for r in range(1, 8):
        total = total + pltpu.roll(folded[pl.ds(r, groups, stride=8), :], span - r, 1)
    partial[...] = total.reshape(partial.shape)

    def rs_copy(to, sender):
        return pltpu.make_async_remote_copy(
            src_ref=partial.at[to], dst_ref=arrived.at[sender],
            send_sem=rs_send.at[to], recv_sem=rs_recv.at[sender],
            device_id=(to, slab), device_id_type=MESH)

    def ag_copy(to, sender):
        return pltpu.make_async_remote_copy(
            src_ref=reduced, dst_ref=gathered.at[sender],
            send_sem=ag_send.at[to], recv_sem=ag_recv.at[sender],
            device_id=(to, slab), device_id_type=MESH)

    def sq_copy(to, sender):
        return pltpu.make_async_remote_copy(
            src_ref=own_sq, dst_ref=all_sq.at[sender],
            send_sem=sq_send.at[to], recv_sem=sq_recv.at[sender],
            device_id=(me, to), device_id_type=MESH)

    @pl.loop(1, n_ctx)
    def _(i):
        rs_copy(ctx_peer(i), me).start()

    arrived[me] = partial[me]

    @pl.loop(0, channels // WIDE)
    def _(c):
        at = pl.ds(pl.multiple_of(c * WIDE, WIDE), WIDE)
        rows = []
        for j in range(per_chunk):
            mine = pl.ds(pl.multiple_of(c * WIDE + j * G, G), G)
            y = rows_dot(windows(gt, mine), toep[c * per_chunk + j])
            rows.append(jnp.concatenate(
                [y[n * G:(n + 1) * G] for n in range(blocks)], axis=1))
        back = jnp.concatenate(rows, axis=0).astype(BF16).T
        gk_ref[:, at] = times(back, v_ref[:, at])
        gv_ref[:, at] = times(back, k_ref[:, at])

    @pl.loop(1, n_ctx)
    def _(i):
        rs_copy(me, ctx_peer(i)).wait_recv()

    reduced[...] = jnp.sum(arrived[...], axis=0)

    @pl.loop(1, n_ctx)
    def _(i):
        ag_copy(ctx_peer(i), me).start()

    gathered[me] = reduced[...]

    @pl.when(me > 0)
    def _():
        for i in range(PARTS):
            p_copy(i).wait_recv()

    @pl.loop(0, channels // WIDE)
    def _(c):
        at = pl.ds(pl.multiple_of(c * WIDE, WIDE), WIDE)
        pt[at, 0:span] = phalo[:, at].T
        rows = []
        for j in range(per_chunk):
            mine = pl.ds(pl.multiple_of(c * WIDE + j * G, G), G)
            u = toep[c * per_chunk + j]
            turned = jnp.concatenate([u[:, span:], u[:, :span]], axis=0)
            y = jnp.dot(windows(pt, mine), turned, preferred_element_type=F32)
            rows.append(jnp.concatenate(
                [y[n * G:(n + 1) * G] for n in range(blocks)], axis=1))
        conv = jnp.concatenate(rows, axis=0).astype(BF16).T
        mix_ref[:, at] = times(conv, q_ref[:, at])
        gq_ref[:, at] = times(conv, g_ref[:, at])

    @pl.loop(1, n_ctx)
    def _(i):
        ag_copy(me, ctx_peer(i)).wait_recv()

    raw = gathered[...].reshape(groups, span)
    squares = jnp.sum(jnp.sum(raw * raw, axis=0, keepdims=True), axis=1, keepdims=True)
    own_sq[...] = jnp.broadcast_to(squares, own_sq.shape)

    @pl.loop(1, n_mp)
    def _(i):
        sq_copy(mp_peer(i), slab).start()

    all_sq[slab] = own_sq[...]

    @pl.loop(1, n_mp)
    def _(i):
        sq_copy(slab, mp_peer(i)).wait_recv()

    square_sum = jnp.sum(all_sq[...], axis=0)[0:1, :]
    grad_rms = jnp.sqrt(square_sum / (groups * n_mp * span) + 1e-06)
    gf_ref[...] = raw * jnp.minimum(1.0, 1.0 / grad_rms)

    for i in range(PARTS):
        @pl.when(me > 0)
        def _():
            g_copy(i).wait_send()

        @pl.when(me < n_ctx - 1)
        def _():
            p_copy(i).wait_send()

    @pl.loop(1, n_ctx)
    def _(i):
        rs_copy(ctx_peer(i), me).wait_send()
        ag_copy(ctx_peer(i), me).wait_send()

    @pl.loop(1, n_mp)
    def _(i):
        sq_copy(mp_peer(i), slab).wait_send()


def shards(queries, key_feats, value_feats, filters, grad_out):
    n_ctx, n_mp = lax.axis_size("ctx"), lax.axis_size("mp")
    tokens, channels = queries.shape
    groups, span = filters.shape
    own = groups // n_ctx
    vmem = pl.BlockSpec(memory_space=pltpu.VMEM)
    dma = pltpu.SemaphoreType.DMA
    like = jax.ShapeDtypeStruct((tokens, channels), BF16)
    return pl.pallas_call(
        functools.partial(kernel, n_ctx, n_mp),
        out_shape=(like, like, like, like, jax.ShapeDtypeStruct((groups, span), F32)),
        in_specs=[vmem] * 5,
        out_specs=[vmem] * 5,
        scratch_shapes=[
            pltpu.VMEM((tokens, channels), BF16),
            pltpu.VMEM((tokens, channels), BF16),
            pltpu.VMEM((span, channels), BF16),
            pltpu.VMEM((span, channels), BF16),
            pltpu.VMEM((groups, span), F32),
            pltpu.VMEM((groups, span, 2 * span), BF16),
            pltpu.VMEM((channels, tokens + span), BF16),
            pltpu.VMEM((channels, tokens + span), BF16),
            pltpu.VMEM((8 * groups, span), F32),
            pltpu.VMEM((n_ctx, own, span), F32),
            pltpu.VMEM((n_ctx, own, span), F32),
            pltpu.VMEM((own, span), F32),
            pltpu.VMEM((n_ctx, own, span), F32),
            pltpu.VMEM((8, span), F32),
            pltpu.VMEM((n_mp, 8, span), F32),
            dma((PARTS,)), dma((PARTS,)), dma((PARTS,)), dma((PARTS,)),
            dma((n_ctx,)), dma((n_ctx,)), dma((n_ctx,)), dma((n_ctx,)),
            dma((n_mp,)), dma((n_mp,)),
        ],
        compiler_params=pltpu.CompilerParams(
            collective_id=0, has_side_effects=True, vmem_limit_bytes=56 * 2**20),
    )(queries, key_feats, value_feats, filters, grad_out)


def solution(mesh):
    placed = (P("ctx", "mp"), P("ctx", "mp"), P("ctx", "mp"), P("mp", None), P("ctx", "mp"))
    return jax.shard_map(
        shards,
        mesh=mesh,
        in_specs=placed,
        out_specs=(P("ctx", "mp"), P("ctx", "mp"), P("ctx", "mp"), P("ctx", "mp"), P("mp", None)),
        check_vma=False,
    )
```

time: 123 us -> 108 us (0.88)
  Pallas kernels: 0 us -> 100 us
  blocking collectives: 59.7 us -> 0 us
  other arithmetic: 15.3 us -> 0 us
  local copies, waits for them, and re-layouts: 21.6 us -> 7.2 us
  waiting for transfers between devices: 12.7 us -> 0 us
  starting transfers between devices: 9.58 us -> 0 us
  matrix products: 2.25 us -> 0 us
    pallas_call x0 -> x1, Pallas kernels: none -> 100 us  [shards(): pl.pallas_call(functools.partial(kernel, n_ctx, n_mp), out_shape=(like, l...]
    all_to_all x2 -> x0, blocking collectives: 35.6 us -> none  [the longest x1 17.8 us: shards(): lax.all_to_all(conv_grad, 'ctx', split_axis=1, concat_axis=0, tiled=True)]
    psum x1 -> x0, blocking collectives: 13 us -> none  [shards(): square_sum = lax.psum(jnp.sum(raw_filters * raw_filters), 'mp')]
    all_to_all x2 -> x0, waiting for transfers between devices: 12.7 us -> none  [the longest x1 12.7 us: shards(): lax.all_to_all(grad_mix, 'ctx', split_axis=0, concat_axis=1, tiled=True)]
    convert_element_type x5 -> x0, other arithmetic: 11.8 us -> none  [the longest x1 3.98 us: shards(): grad_values = (back_f * key_feats.astype(jnp.float32)).astype(jnp.bfloat16)]
    all_gather x1 -> x0, blocking collectives: 11.1 us -> none  [shards(): raw_filters = lax.all_gather(partial_grad, 'ctx', axis=0, tiled=True)]
    all_to_all x2 -> x0, starting transfers between devices: 9.58 us -> none  [the longest x1 5.17 us: shards(): lax.all_to_all(grad_mix, 'ctx', split_axis=0, concat_axis=1, tiled=True)]
    convert_element_type x6 -> x0, local copies, waits for them, and re-layouts: 6.1 us -> none  [the longest x1 2.01 us: shards(): conv_f = conv_rows.T.astype(jnp.float32)]
  transfers between devices with their start and end apart: 2 -> 0, of which waited for: 1 -> 0; matrix products, arithmetic and copies ran while one was open for 9% -> 0% of each run, Pallas kernels for 0% -> 0%
where the time goes in v1:
time: 108 us
  Pallas kernels  100 us (93%)
  local copies, waits for them, and re-layouts  7.2 us (7%)
    pallas_call x1, Pallas kernels, shards(): pl.pallas_call(functools.partial(kernel, n_ctx, n_mp), out_shape=(like, l...  100 us
    unnamed x13, local copies, waits for them, and re-layouts  7.2 us

profile of v1, /device:TPU:0, one launch (start us, length us, event | category | flops | bytes accessed | tf_op | source)
XLA Modules:
  0.0 107.8 jit_solution(1147144764182282318)
XLA Ops:
  0.6 100.0 %shard_map.92 = (bf16[256,2048]{1,0:T(8,128)(2,1)}, bf16[256,2048]{1,0:T(8,128)(2,1)}, bf16[256,2048]{1,0:T(8,128)(2,1)}, bf16[256,2048]{1,0:T(8,128)(2,1)}, f32[128,128]{1,0:T(8,128)}) custom-call(bf16[256,2048]{1,0:T(8,128)(2,1)} %q_ref.1, bf16[256,2048]{1,0:T(8,128)(2,1)} %k_ref.1, bf16[256,2048]{1,0:T(8,128)(2,1)} %v_ref.1, bf16[128,128]{1,0:T(8,128)(2,1)} %f_ref.1, ...), custom_call_target="tpu_custom_call" | custom-call | tf_op jit(solution)/shard_map/pallas_call | solution.py:270
  100.6 0.0 copy-start.2
  100.6 2.4 %copy.15 = bf16[256,2048]{1,0:T(8,128)(2,1)} copy(bf16[256,2048]{1,0:T(8,128)(2,1)} %get-tuple-element.10) | data formatting | bytes 2097152
  103.0 0.0 copy-done.2
  103.0 0.0 copy-start.1
  103.0 1.0 copy.16
  104.0 0.6 copy-done.1
  104.6 0.0 copy-start
  104.6 1.0 copy.17
  105.6 0.6 copy-done
  106.2 0.0 copy-start.3
  106.2 1.0 copy.18
  107.2 0.0 copy-done.3
  107.2 0.6 copy.19
Async XLA Ops:
  100.6 2.4 %copy-start.2 = (bf16[256,2048]{1,0:T(8,128)(2,1)S(1)}, bf16[256,2048]{1,0:T(8,128)(2,1)}, u32[]{:S(2)}) copy-start(bf16[256,2048]{1,0:T(8,128)(2,1)} %get-tuple-element.11) | copy-start | bytes 3145732
  103.0 1.6 %copy-start.1 = (bf16[256,2048]{1,0:T(8,128)(2,1)S(1)}, bf16[256,2048]{1,0:T(8,128)(2,1)}, u32[]{:S(2)}) copy-start(bf16[256,2048]{1,0:T(8,128)(2,1)} %get-tuple-element.12) | copy-start | bytes 3145732
  104.6 1.6 %copy-start = (bf16[256,2048]{1,0:T(8,128)(2,1)S(1)}, bf16[256,2048]{1,0:T(8,128)(2,1)}, u32[]{:S(2)}) copy-start(bf16[256,2048]{1,0:T(8,128)(2,1)} %get-tuple-element.13) | copy-start | bytes 3145732
  106.2 1.0 copy-start.3

commit v2 on v1

--- a/solution.py
+++ b/solution.py
@@ -19,13 +19,9 @@
     return (a.astype(F32) * b.astype(F32)).astype(BF16)
 
 
-def rows_dot(a, b):
-    return lax.dot_general(a, b, (((1,), (1,)), ((), ())), preferred_element_type=F32)
-
-
 def kernel(n_ctx, n_mp, q_ref, k_ref, v_ref, f_ref, g_ref,
            mix_ref, gq_ref, gk_ref, gv_ref, gf_ref,
-           prod, gmix, phalo, ghalo, taps, toep, pt, gt, folded,
+           prod, gmix, phalo, ghalo, taps, flipped, toep, toep_f, folded,
            partial, arrived, reduced, gathered, own_sq, all_sq,
            p_send, p_recv, g_send, g_recv,
            rs_send, rs_recv, ag_send, ag_recv, sq_send, sq_recv):
@@ -99,19 +95,45 @@
     row = lax.broadcasted_iota(jnp.int32, (span, span), 0)
     upper = col >= row
 
-    @pl.loop(0, groups)
-    def _(i):
-        line = jnp.broadcast_to(taps[pl.ds(i, 1), :], (span, span))
+    flip = jnp.where(lax.rem(row + col, span) == 0, 1.0, 0.0).astype(BF16)
+    flipped[...] = jnp.dot(f_ref[...], flip, preferred_element_type=F32)
+
+    def spread(i, lines, out, mask):
+        line = jnp.broadcast_to(lines[pl.ds(i, 1), :], (span, span))
         turned = pltpu.roll(line, 0, 1, stride=1, stride_axis=0)
         zero = jnp.zeros_like(turned)
-        toep[i, :, 0:span] = jnp.where(upper, turned, zero).astype(BF16)
-        toep[i, :, span:] = jnp.where(upper, zero, turned).astype(BF16)
-
-    @pl.loop(0, channels // WIDE)
+        out[i, :, 0:span] = jnp.where(mask, turned, zero).astype(BF16)
+        out[i, :, span:] = jnp.where(mask, zero, turned).astype(BF16)
+
+    @pl.loop(0, groups // per_chunk)
     def _(c):
-        at = pl.ds(pl.multiple_of(c * WIDE, WIDE), WIDE)
-        pt[at, span:] = prod[:, at].T
-        gt[at, 0:tokens] = gmix[:, at].T
+        for j in range(per_chunk):
+            spread(c * per_chunk + j, taps, toep, upper)
+            spread(c * per_chunk + j, flipped, toep_f, col > row)
+
+    lane = lax.broadcasted_iota(jnp.int32, (1, blocks * WIDE), 1)
+    member = lax.rem(lane, WIDE) // G
+
+    def g_windows(at):
+        own_part = gmix[:, at]
+        last = jnp.concatenate([gmix[tail, at], ghalo[:, at]], axis=0)
+        wins = [own_part[n * span:(n + 2) * span] for n in range(blocks - 1)]
+        return jnp.concatenate(wins + [last], axis=1)
+
+    def p_windows(at):
+        own_part = prod[:, at]
+        first = jnp.concatenate([phalo[:, at], prod[head, at]], axis=0)
+        wins = [own_part[(n - 1) * span:(n + 1) * span] for n in range(1, blocks)]
+        return jnp.concatenate([first] + wins, axis=1)
+
+    def conv(c, mats, wins):
+        out = None
+        for j in range(per_chunk):
+            y = jnp.dot(mats[c * per_chunk + j], wins, preferred_element_type=F32)
+            out = y if out is None else jnp.where(member == j, y, out)
+        out = out.astype(BF16)
+        return jnp.concatenate(
+            [out[:, n * WIDE:(n + 1) * WIDE] for n in range(blocks)], axis=0)
 
     @pl.when(me < n_ctx - 1)
     def _():
@@ -121,27 +143,18 @@
     @pl.loop(0, channels // WIDE)
     def _(c):
         at = pl.ds(pl.multiple_of(c * WIDE, WIDE), WIDE)
-        gt[at, tokens:] = ghalo[:, at].T
-
-    def windows(ref, at):
-        x = ref[at, :]
-        return jnp.concatenate(
-            [x[:, n * span:(n + 2) * span] for n in range(blocks)], axis=0)
-
-    @pl.loop(0, groups)
-    def _(i):
-        at = pl.ds(pl.multiple_of(i * G, G), G)
-        x = pt[at, :]
+        wins = g_windows(at).T
         left = jnp.concatenate(
-            [x[:, (n + 1) * span:(n + 2) * span] for n in range(blocks)], axis=0)
-        both = lax.dot_general(left, windows(gt, at), (((0,), (0,)), ((), ())),
-                               preferred_element_type=F32)
-        turn = jnp.where(upper, both[:, :span], both[:, span:])
-        half = span // 2
-        while half >= 8:
-            turn = turn[:half] + pltpu.roll(turn[half:], span - half, 1)
-            half //= 2
-        folded[pl.ds(pl.multiple_of(i * 8, 8), 8), :] = turn
+            [prod[n * span:(n + 1) * span, at] for n in range(blocks)], axis=1)
+        for j in range(per_chunk):
+            mine = jnp.where(member == j, left, jnp.zeros_like(left))
+            both = jnp.dot(mine, wins, preferred_element_type=F32)
+            turn = jnp.where(upper, both[:, :span], both[:, span:])
+            half = span // 2
+            while half >= 8:
+                turn = turn[:half] + pltpu.roll(turn[half:], span - half, 1)
+                half //= 2
+            folded[pl.ds(pl.multiple_of((c * per_chunk + j) * 8, 8), 8), :] = turn
 
     total = folded[pl.ds(0, groups, stride=8), :]
     for r in range(1, 8):
@@ -175,13 +188,7 @@
     @pl.loop(0, channels // WIDE)
     def _(c):
         at = pl.ds(pl.multiple_of(c * WIDE, WIDE), WIDE)
-        rows = []
-        for j in range(per_chunk):
-            mine = pl.ds(pl.multiple_of(c * WIDE + j * G, G), G)
-            y = rows_dot(windows(gt, mine), toep[c * per_chunk + j])
-            rows.append(jnp.concatenate(
-                [y[n * G:(n + 1) * G] for n in range(blocks)], axis=1))
-        back = jnp.concatenate(rows, axis=0).astype(BF16).T
+        back = conv(c, toep, g_windows(at))
         gk_ref[:, at] = times(back, v_ref[:, at])
         gv_ref[:, at] = times(back, k_ref[:, at])
 
@@ -205,18 +212,9 @@
     @pl.loop(0, channels // WIDE)
     def _(c):
         at = pl.ds(pl.multiple_of(c * WIDE, WIDE), WIDE)
-        pt[at, 0:span] = phalo[:, at].T
-        rows = []
-        for j in range(per_chunk):
-            mine = pl.ds(pl.multiple_of(c * WIDE + j * G, G), G)
-            u = toep[c * per_chunk + j]
-            turned = jnp.concatenate([u[:, span:], u[:, :span]], axis=0)
-            y = jnp.dot(windows(pt, mine), turned, preferred_element_type=F32)
-            rows.append(jnp.concatenate(
-                [y[n * G:(n + 1) * G] for n in range(blocks)], axis=1))
-        conv = jnp.concatenate(rows, axis=0).astype(BF16).T
-        mix_ref[:, at] = times(conv, q_ref[:, at])
-        gq_ref[:, at] = times(conv, g_ref[:, at])
+        ahead = conv(c, toep_f, p_windows(at))
+        mix_ref[:, at] = times(ahead, q_ref[:, at])
+        gq_ref[:, at] = times(ahead, g_ref[:, at])
 
     @pl.loop(1, n_ctx)
     def _(i):
@@ -278,9 +276,9 @@
             pltpu.VMEM((span, channels), BF16),
             pltpu.VMEM((span, channels), BF16),
             pltpu.VMEM((groups, span), F32),
+            pltpu.VMEM((groups, span), F32),
             pltpu.VMEM((groups, span, 2 * span), BF16),
-            pltpu.VMEM((channels, tokens + span), BF16),
-            pltpu.VMEM((channels, tokens + span), BF16),
+            pltpu.VMEM((groups, span, 2 * span), BF16),
             pltpu.VMEM((8 * groups, span), F32),
             pltpu.VMEM((n_ctx, own, span), F32),
             pltpu.VMEM((n_ctx, own, span), F32),

time: 108 us -> 57.2 us (0.53)
  the two profiles are of different devices: /device:TPU:0 before, /device:TPU:1 now
where the time goes in v2:
time: 57.2 us; the launch traced here: 57 us
  Pallas kernels  49.1 us (86%)
  local copies, waits for them, and re-layouts  7.2 us (13%)
  between operations  0.65 us (1%)
    pallas_call x1, Pallas kernels, shards(): pl.pallas_call(functools.partial(kernel, n_ctx, n_mp), out_shape=(like, l...  49.1 us
    unnamed x13, local copies, waits for them, and re-layouts  7.2 us

profile of v2, /device:TPU:1, one launch (start us, length us, event | category | flops | bytes accessed | tf_op | source)
XLA Modules:
  0.0 57.0 jit_solution(7445875224667751496)
XLA Ops:
  0.6 49.1 %shard_map.92 = (bf16[256,2048]{1,0:T(8,128)(2,1)}, bf16[256,2048]{1,0:T(8,128)(2,1)}, bf16[256,2048]{1,0:T(8,128)(2,1)}, bf16[256,2048]{1,0:T(8,128)(2,1)}, f32[128,128]{1,0:T(8,128)}) custom-call(bf16[256,2048]{1,0:T(8,128)(2,1)} %q_ref.1, bf16[256,2048]{1,0:T(8,128)(2,1)} %k_ref.1, bf16[256,2048]{1,0:T(8,128)(2,1)} %v_ref.1, bf16[128,128]{1,0:T(8,128)(2,1)} %f_ref.1, ...), custom_call_target="tpu_custom_call" | custom-call | tf_op jit(solution)/shard_map/pallas_call | solution.py:268
  49.7 0.0 copy-start.2
  49.7 2.4 %copy.15 = bf16[256,2048]{1,0:T(8,128)(2,1)} copy(bf16[256,2048]{1,0:T(8,128)(2,1)} %get-tuple-element.10) | data formatting | bytes 2097152
  52.1 0.0 copy-done.2
  52.1 0.0 copy-start.1
  52.1 1.0 %copy.16 = bf16[256,2048]{1,0:T(8,128)(2,1)} copy(bf16[256,2048]{1,0:T(8,128)(2,1)S(1)} %copy-done.2) | data formatting | bytes 2097152
  53.1 0.6 %copy-done.1 = bf16[256,2048]{1,0:T(8,128)(2,1)S(1)} copy-done((bf16[256,2048]{1,0:T(8,128)(2,1)S(1)}, bf16[256,2048]{1,0:T(8,128)(2,1)}, u32[]{:S(2)}) %copy-start.1) | copy-done | bytes 1048600
  53.7 0.0 copy-start
  53.7 1.0 %copy.17 = bf16[256,2048]{1,0:T(8,128)(2,1)} copy(bf16[256,2048]{1,0:T(8,128)(2,1)S(1)} %copy-done.1) | data formatting | bytes 2097152
  54.7 0.6 %copy-done = bf16[256,2048]{1,0:T(8,128)(2,1)S(1)} copy-done((bf16[256,2048]{1,0:T(8,128)(2,1)S(1)}, bf16[256,2048]{1,0:T(8,128)(2,1)}, u32[]{:S(2)}) %copy-start) | copy-done | bytes 1048600
  55.4 0.0 copy-start.3
  55.4 1.0 %copy.18 = bf16[256,2048]{1,0:T(8,128)(2,1)} copy(bf16[256,2048]{1,0:T(8,128)(2,1)S(1)} %copy-done) | data formatting | bytes 2097152
  56.3 0.0 copy-done.3
  56.3 0.6 %copy.19 = f32[128,128]{1,0:T(8,128)} copy(f32[128,128]{1,0:T(8,128)S(1)} %copy-done.3) | data formatting | bytes 131072
Async XLA Ops:
  49.7 2.4 %copy-start.2 = (bf16[256,2048]{1,0:T(8,128)(2,1)S(1)}, bf16[256,2048]{1,0:T(8,128)(2,1)}, u32[]{:S(2)}) copy-start(bf16[256,2048]{1,0:T(8,128)(2,1)} %get-tuple-element.11) | copy-start | bytes 3145732
  52.1 1.6 %copy-start.1 = (bf16[256,2048]{1,0:T(8,128)(2,1)S(1)}, bf16[256,2048]{1,0:T(8,128)(2,1)}, u32[]{:S(2)}) copy-start(bf16[256,2048]{1,0:T(8,128)(2,1)} %get-tuple-element.12) | copy-start | bytes 3145732
  53.7 1.6 %copy-start = (bf16[256,2048]{1,0:T(8,128)(2,1)S(1)}, bf16[256,2048]{1,0:T(8,128)(2,1)}, u32[]{:S(2)}) copy-start(bf16[256,2048]{1,0:T(8,128)(2,1)} %get-tuple-element.13) | copy-start | bytes 3145732
  55.4 1.0 %copy-start.3 = (f32[128,128]{1,0:T(8,128)S(1)}, f32[128,128]{1,0:T(8,128)}, u32[]{:S(2)}) copy-start(f32[128,128]{1,0:T(8,128)} %get-tuple-element.14) | copy-start | bytes 196612

commit v3 on v2

--- a/solution.py
+++ b/solution.py
@@ -127,10 +127,12 @@
         return jnp.concatenate([first] + wins, axis=1)
 
     def conv(c, mats, wins):
-        out = None
-        for j in range(per_chunk):
-            y = jnp.dot(mats[c * per_chunk + j], wins, preferred_element_type=F32)
-            out = y if out is None else jnp.where(member == j, y, out)
+        stack = mats[pl.ds(pl.multiple_of(c * per_chunk, per_chunk), per_chunk)]
+        y = jnp.dot(stack.reshape(per_chunk * span, 2 * span), wins,
+                    preferred_element_type=F32)
+        out = y[:span]
+        for j in range(1, per_chunk):
+            out = jnp.where(member == j, y[j * span:(j + 1) * span], out)
         out = out.astype(BF16)
         return jnp.concatenate(
             [out[:, n * WIDE:(n + 1) * WIDE] for n in range(blocks)], axis=0)
@@ -146,9 +148,11 @@
         wins = g_windows(at).T
         left = jnp.concatenate(
             [prod[n * span:(n + 1) * span, at] for n in range(blocks)], axis=1)
+        mine = jnp.concatenate(
+            [jnp.where(member == j, left, jnp.zeros_like(left)) for j in range(per_chunk)], axis=0)
+        every = jnp.dot(mine, wins, preferred_element_type=F32)
         for j in range(per_chunk):
-            mine = jnp.where(member == j, left, jnp.zeros_like(left))
-            both = jnp.dot(mine, wins, preferred_element_type=F32)
+            both = every[j * span:(j + 1) * span]
             turn = jnp.where(upper, both[:, :span], both[:, span:])
             half = span // 2
             while half >= 8:
@@ -185,36 +189,36 @@
 
     arrived[me] = partial[me]
 
-    @pl.loop(0, channels // WIDE)
-    def _(c):
-        at = pl.ds(pl.multiple_of(c * WIDE, WIDE), WIDE)
-        back = conv(c, toep, g_windows(at))
-        gk_ref[:, at] = times(back, v_ref[:, at])
-        gv_ref[:, at] = times(back, k_ref[:, at])
-
-    @pl.loop(1, n_ctx)
-    def _(i):
-        rs_copy(me, ctx_peer(i)).wait_recv()
-
-    reduced[...] = jnp.sum(arrived[...], axis=0)
-
-    @pl.loop(1, n_ctx)
-    def _(i):
-        ag_copy(ctx_peer(i), me).start()
-
-    gathered[me] = reduced[...]
-
     @pl.when(me > 0)
     def _():
         for i in range(PARTS):
             p_copy(i).wait_recv()
 
-    @pl.loop(0, channels // WIDE)
-    def _(c):
+    def both_convs(c):
         at = pl.ds(pl.multiple_of(c * WIDE, WIDE), WIDE)
+        back = conv(c, toep, g_windows(at))
         ahead = conv(c, toep_f, p_windows(at))
+        gk_ref[:, at] = times(back, v_ref[:, at])
+        gv_ref[:, at] = times(back, k_ref[:, at])
         mix_ref[:, at] = times(ahead, q_ref[:, at])
         gq_ref[:, at] = times(ahead, g_ref[:, at])
+
+    chunks = channels // WIDE
+    pl.loop(0, chunks // 2)(both_convs)
+
+    @pl.loop(1, n_ctx)
+    def _(i):
+        rs_copy(me, ctx_peer(i)).wait_recv()
+
+    reduced[...] = jnp.sum(arrived[...], axis=0)
+
+    @pl.loop(1, n_ctx)
+    def _(i):
+        ag_copy(ctx_peer(i), me).start()
+
+    gathered[me] = reduced[...]
+
+    pl.loop(chunks // 2, chunks)(both_convs)
 
     @pl.loop(1, n_ctx)
     def _(i):

time: 57.2 us -> 52.7 us (0.921)
  the two profiles are of different devices: /device:TPU:1 before, /device:TPU:0 now
where the time goes in v3:
time: 52.7 us; the launch traced here: 51.7 us
  Pallas kernels  43.8 us (83%)
  local copies, waits for them, and re-layouts  7.2 us (14%)
  between operations  0.65 us (1%)
    pallas_call x1, Pallas kernels, shards(): pl.pallas_call(functools.partial(kernel, n_ctx, n_mp), out_shape=(like, l...  43.8 us
    unnamed x13, local copies, waits for them, and re-layouts  7.2 us

profile of v3, /device:TPU:0, one launch (start us, length us, event | category | flops | bytes accessed | tf_op | source)
XLA Modules:
  0.0 51.7 jit_solution(8498194797775662666)
XLA Ops:
  0.6 43.8 %shard_map.92 = (bf16[256,2048]{1,0:T(8,128)(2,1)}, bf16[256,2048]{1,0:T(8,128)(2,1)}, bf16[256,2048]{1,0:T(8,128)(2,1)}, bf16[256,2048]{1,0:T(8,128)(2,1)}, f32[128,128]{1,0:T(8,128)}) custom-call(bf16[256,2048]{1,0:T(8,128)(2,1)} %q_ref.1, bf16[256,2048]{1,0:T(8,128)(2,1)} %k_ref.1, bf16[256,2048]{1,0:T(8,128)(2,1)} %v_ref.1, bf16[128,128]{1,0:T(8,128)(2,1)} %f_ref.1, ...), custom_call_target="tpu_custom_call" | custom-call | tf_op jit(solution)/shard_map/pallas_call | solution.py:272
  44.5 0.0 copy-start.2
  44.5 2.4 %copy.15 = bf16[256,2048]{1,0:T(8,128)(2,1)} copy(bf16[256,2048]{1,0:T(8,128)(2,1)} %get-tuple-element.10) | data formatting | bytes 2097152
  46.9 0.0 copy-done.2
  46.9 0.0 copy-start.1
  46.9 1.0 %copy.16 = bf16[256,2048]{1,0:T(8,128)(2,1)} copy(bf16[256,2048]{1,0:T(8,128)(2,1)S(1)} %copy-done.2) | data formatting | bytes 2097152
  47.8 0.6 %copy-done.1 = bf16[256,2048]{1,0:T(8,128)(2,1)S(1)} copy-done((bf16[256,2048]{1,0:T(8,128)(2,1)S(1)}, bf16[256,2048]{1,0:T(8,128)(2,1)}, u32[]{:S(2)}) %copy-start.1) | copy-done | bytes 1048600
  48.5 0.0 copy-start
  48.5 1.0 %copy.17 = bf16[256,2048]{1,0:T(8,128)(2,1)} copy(bf16[256,2048]{1,0:T(8,128)(2,1)S(1)} %copy-done.1) | data formatting | bytes 2097152
  49.4 0.6 %copy-done = bf16[256,2048]{1,0:T(8,128)(2,1)S(1)} copy-done((bf16[256,2048]{1,0:T(8,128)(2,1)S(1)}, bf16[256,2048]{1,0:T(8,128)(2,1)}, u32[]{:S(2)}) %copy-start) | copy-done | bytes 1048600
  50.1 0.0 copy-start.3
  50.1 1.0 %copy.18 = bf16[256,2048]{1,0:T(8,128)(2,1)} copy(bf16[256,2048]{1,0:T(8,128)(2,1)S(1)} %copy-done) | data formatting | bytes 2097152
  51.0 0.0 copy-done.3
  51.0 0.6 %copy.19 = f32[128,128]{1,0:T(8,128)} copy(f32[128,128]{1,0:T(8,128)S(1)} %copy-done.3) | data formatting | bytes 131072
Async XLA Ops:
  44.5 2.4 %copy-start.2 = (bf16[256,2048]{1,0:T(8,128)(2,1)S(1)}, bf16[256,2048]{1,0:T(8,128)(2,1)}, u32[]{:S(2)}) copy-start(bf16[256,2048]{1,0:T(8,128)(2,1)} %get-tuple-element.11) | copy-start | bytes 3145732
  46.9 1.6 %copy-start.1 = (bf16[256,2048]{1,0:T(8,128)(2,1)S(1)}, bf16[256,2048]{1,0:T(8,128)(2,1)}, u32[]{:S(2)}) copy-start(bf16[256,2048]{1,0:T(8,128)(2,1)} %get-tuple-element.12) | copy-start | bytes 3145732
  48.5 1.6 %copy-start = (bf16[256,2048]{1,0:T(8,128)(2,1)S(1)}, bf16[256,2048]{1,0:T(8,128)(2,1)}, u32[]{:S(2)}) copy-start(bf16[256,2048]{1,0:T(8,128)(2,1)} %get-tuple-element.13) | copy-start | bytes 3145732
  50.1 1.0 %copy-start.3 = (f32[128,128]{1,0:T(8,128)S(1)}, f32[128,128]{1,0:T(8,128)}, u32[]{:S(2)}) copy-start(f32[128,128]{1,0:T(8,128)} %get-tuple-element.14) | copy-start | bytes 196612

commit v4 on v3

--- a/solution.py
+++ b/solution.py
@@ -129,11 +129,10 @@
     def conv(c, mats, wins):
         stack = mats[pl.ds(pl.multiple_of(c * per_chunk, per_chunk), per_chunk)]
         y = jnp.dot(stack.reshape(per_chunk * span, 2 * span), wins,
-                    preferred_element_type=F32)
+                    preferred_element_type=F32).astype(BF16)
         out = y[:span]
         for j in range(1, per_chunk):
             out = jnp.where(member == j, y[j * span:(j + 1) * span], out)
-        out = out.astype(BF16)
         return jnp.concatenate(
             [out[:, n * WIDE:(n + 1) * WIDE] for n in range(blocks)], axis=0)
 
@@ -268,10 +267,10 @@
     own = groups // n_ctx
     vmem = pl.BlockSpec(memory_space=pltpu.VMEM)
     dma = pltpu.SemaphoreType.DMA
-    like = jax.ShapeDtypeStruct((tokens, channels), BF16)
+    like = pltpu.VMEM((tokens, channels), BF16)
     return pl.pallas_call(
         functools.partial(kernel, n_ctx, n_mp),
-        out_shape=(like, like, like, like, jax.ShapeDtypeStruct((groups, span), F32)),
+        out_shape=(like, like, like, like, pltpu.VMEM((groups, span), F32)),
         in_specs=[vmem] * 5,
         out_specs=[vmem] * 5,
         scratch_shapes=[

time: 52.7 us -> 47.8 us (0.907)
  local copies, waits for them, and re-layouts: 7.2 us -> 4.51 us
  Pallas kernels: 43.8 us -> 41.8 us
    unnamed x13 -> x5, local copies, waits for them, and re-layouts: 7.2 us -> 4.51 us
    pallas_call x1, Pallas kernels: 43.8 us -> 41.8 us  [shards(): pl.pallas_call(functools.partial(kernel, n_ctx, n_mp), out_shape=(like, l...]
where the time goes in v4:
time: 47.8 us; the launch traced here: 47 us
  Pallas kernels  41.8 us (87%)
  local copies, waits for them, and re-layouts  4.51 us (9%)
  between operations  0.64 us (1%)
    pallas_call x1, Pallas kernels, shards(): pl.pallas_call(functools.partial(kernel, n_ctx, n_mp), out_shape=(like, l...  41.8 us
    unnamed x5, local copies, waits for them, and re-layouts  4.51 us

profile of v4, /device:TPU:0, one launch (start us, length us, event | category | flops | bytes accessed | tf_op | source)
XLA Modules:
  0.0 47.0 jit_solution(15551811234603184662)
XLA Ops:
  0.6 41.8 %shard_map.92 = (bf16[256,2048]{1,0:T(8,128)(2,1)S(1)}, bf16[256,2048]{1,0:T(8,128)(2,1)S(1)}, bf16[256,2048]{1,0:T(8,128)(2,1)S(1)}, bf16[256,2048]{1,0:T(8,128)(2,1)S(1)}, f32[128,128]{1,0:T(8,128)S(1)}) custom-call(bf16[256,2048]{1,0:T(8,128)(2,1)} %q_ref.1, bf16[256,2048]{1,0:T(8,128)(2,1)} %k_ref.1, bf16[256,2048]{1,0:T(8,128)(2,1)} %v_ref.1, ...), custom_call_target="tpu_custom_call" | custom-call | tf_op jit(solution)/shard_map/pallas_call | solution.py:271
  42.5 1.0 %copy.15 = bf16[256,2048]{1,0:T(8,128)(2,1)} copy(bf16[256,2048]{1,0:T(8,128)(2,1)S(1)} %get-tuple-element.5) | data formatting | bytes 2097152
  43.4 0.6 %copy.19 = f32[128,128]{1,0:T(8,128)} copy(f32[128,128]{1,0:T(8,128)S(1)} %get-tuple-element.9) | data formatting | bytes 131072
  44.1 1.0 %copy.16 = bf16[256,2048]{1,0:T(8,128)(2,1)} copy(bf16[256,2048]{1,0:T(8,128)(2,1)S(1)} %get-tuple-element.6) | data formatting | bytes 2097152
  45.0 1.0 %copy.17 = bf16[256,2048]{1,0:T(8,128)(2,1)} copy(bf16[256,2048]{1,0:T(8,128)(2,1)S(1)} %get-tuple-element.7) | data formatting | bytes 2097152
  46.0 1.0 %copy.18 = bf16[256,2048]{1,0:T(8,128)(2,1)} copy(bf16[256,2048]{1,0:T(8,128)(2,1)S(1)} %get-tuple-element.8) | data formatting | bytes 2097152

commit v5 on v4

--- a/solution.py
+++ b/solution.py
@@ -12,24 +12,24 @@
 F32 = jnp.float32
 BF16 = jnp.bfloat16
 WIDE = 128
-PARTS = 4
+PART = 256
 
 
 def times(a, b):
     return (a.astype(F32) * b.astype(F32)).astype(BF16)
 
 
-def kernel(n_ctx, n_mp, q_ref, k_ref, v_ref, f_ref, g_ref,
+def kernel(n_ctx, n_mp, q_hbm, k_hbm, v_hbm, f_ref, g_hbm,
            mix_ref, gq_ref, gk_ref, gv_ref, gf_ref,
-           prod, gmix, phalo, ghalo, taps, flipped, toep, toep_f, folded,
+           q_ref, k_ref, v_ref, g_ref, prod, gmix, phalo, ghalo, taps, flipped, toep, toep_f, folded,
            partial, arrived, reduced, gathered, own_sq, all_sq,
            p_send, p_recv, g_send, g_recv,
-           rs_send, rs_recv, ag_send, ag_recv, sq_send, sq_recv):
+           rs_send, rs_recv, ag_send, ag_recv, sq_send, sq_recv, load):
     tokens, channels = q_ref.shape
     groups, span = f_ref.shape
     blocks = tokens // span
     own = groups // n_ctx
-    part = channels // PARTS
+    parts = channels // PART
     me = lax.axis_index("ctx")
     slab = lax.axis_index("mp")
     per_chunk = WIDE // G
@@ -51,25 +51,40 @@
         pl.semaphore_signal(barrier, inc=1, device_id=(me, mp_peer(i)), device_id_type=MESH)
 
     head, tail = slice(0, span), slice(tokens - span, tokens)
+    rest_g, rest_p = slice(span, tokens), slice(0, tokens - span)
+
+    def loads(pairs, first):
+        return [pltpu.make_async_copy(a.at[rows, :], b.at[rows, :], load.at[first + i])
+                for i, (a, b, rows) in enumerate(pairs)]
+
+    edges = loads([(g_hbm, g_ref, head), (q_hbm, q_ref, head),
+                   (k_hbm, k_ref, tail), (v_hbm, v_ref, tail)], 0)
+    others = loads([(g_hbm, g_ref, rest_g), (q_hbm, q_ref, rest_g),
+                    (k_hbm, k_ref, rest_p), (v_hbm, v_ref, rest_p)], 4)
+    for copy in edges + others:
+        copy.start()
+    for copy in edges:
+        copy.wait()
     gmix[head, :] = times(g_ref[head, :], q_ref[head, :])
     prod[tail, :] = times(k_ref[tail, :], v_ref[tail, :])
     pl.semaphore_wait(barrier, n_ctx + n_mp - 2)
 
     def g_copy(i):
-        cols = slice(i * part, (i + 1) * part)
+        cols = pl.ds(pl.multiple_of(i * PART, PART), PART)
         return pltpu.make_async_remote_copy(
             src_ref=gmix.at[head, cols], dst_ref=ghalo.at[:, cols],
             send_sem=g_send.at[i], recv_sem=g_recv.at[i],
             device_id=(lax.rem(me + n_ctx - 1, n_ctx), slab), device_id_type=MESH)
 
     def p_copy(i):
-        cols = slice(i * part, (i + 1) * part)
+        cols = pl.ds(pl.multiple_of(i * PART, PART), PART)
         return pltpu.make_async_remote_copy(
             src_ref=prod.at[tail, cols], dst_ref=phalo.at[:, cols],
             send_sem=p_send.at[i], recv_sem=p_recv.at[i],
             device_id=(lax.rem(me + 1, n_ctx), slab), device_id_type=MESH)
 
-    for i in range(PARTS):
+    @pl.loop(0, parts)
+    def _(i):
         @pl.when(me > 0)
         def _():
             g_copy(i).start()
@@ -86,7 +101,8 @@
     def _():
         ghalo[...] = jnp.zeros_like(ghalo)
 
-    rest_g, rest_p = slice(span, tokens), slice(0, tokens - span)
+    for copy in others:
+        copy.wait()
     gmix[rest_g, :] = times(g_ref[rest_g, :], q_ref[rest_g, :])
     prod[rest_p, :] = times(k_ref[rest_p, :], v_ref[rest_p, :])
     taps[...] = f_ref[...].astype(F32)
@@ -136,13 +152,9 @@
         return jnp.concatenate(
             [out[:, n * WIDE:(n + 1) * WIDE] for n in range(blocks)], axis=0)
 
-    @pl.when(me < n_ctx - 1)
-    def _():
-        for i in range(PARTS):
-            g_copy(i).wait_recv()
-
-    @pl.loop(0, channels // WIDE)
-    def _(c):
+    chunks = PART // WIDE
+
+    def correlate(c):
         at = pl.ds(pl.multiple_of(c * WIDE, WIDE), WIDE)
         wins = g_windows(at).T
         left = jnp.concatenate(
@@ -159,6 +171,15 @@
                 half //= 2
             folded[pl.ds(pl.multiple_of((c * per_chunk + j) * 8, 8), 8), :] = turn
 
+    @pl.loop(0, parts)
+    def _(i):
+        @pl.when(me < n_ctx - 1)
+        def _():
+            g_copy(i).wait_recv()
+
+        for c in range(chunks):
+            correlate(i * chunks + c)
+
     total = folded[pl.ds(0, groups, stride=8), :]
     for r in range(1, 8):
         total = total + pltpu.roll(folded[pl.ds(r, groups, stride=8), :], span - r, 1)
@@ -187,11 +208,6 @@
         rs_copy(ctx_peer(i), me).start()
 
     arrived[me] = partial[me]
-
-    @pl.when(me > 0)
-    def _():
-        for i in range(PARTS):
-            p_copy(i).wait_recv()
 
     def both_convs(c):
         at = pl.ds(pl.multiple_of(c * WIDE, WIDE), WIDE)
@@ -202,8 +218,15 @@
         mix_ref[:, at] = times(ahead, q_ref[:, at])
         gq_ref[:, at] = times(ahead, g_ref[:, at])
 
-    chunks = channels // WIDE
-    pl.loop(0, chunks // 2)(both_convs)
+    def convs(i):
+        @pl.when(me > 0)
+        def _():
+            p_copy(i).wait_recv()
+
+        for c in range(chunks):
+            both_convs(i * chunks + c)
+
+    pl.loop(0, parts // 2)(convs)
 
     @pl.loop(1, n_ctx)
     def _(i):
@@ -217,7 +240,7 @@
 
     gathered[me] = reduced[...]
 
-    pl.loop(chunks // 2, chunks)(both_convs)
+    pl.loop(parts // 2, parts)(convs)
 
     @pl.loop(1, n_ctx)
     def _(i):
@@ -241,7 +264,8 @@
     grad_rms = jnp.sqrt(square_sum / (groups * n_mp * span) + 1e-06)
     gf_ref[...] = raw * jnp.minimum(1.0, 1.0 / grad_rms)
 
-    for i in range(PARTS):
+    @pl.loop(0, parts)
+    def _(i):
         @pl.when(me > 0)
         def _():
             g_copy(i).wait_send()
@@ -258,6 +282,15 @@
     @pl.loop(1, n_mp)
     def _(i):
         sq_copy(mp_peer(i), slab).wait_send()
+
+
+def unload(a, b, c, d, e, ao, bo, co, do, eo, sems):
+    copies = [pltpu.make_async_copy(x, y, sems.at[i]) for i, (x, y) in enumerate(
+        zip((a, b, c, d, e), (ao, bo, co, do, eo)))]
+    for copy in copies:
+        copy.start()
+    for copy in copies:
+        copy.wait()
 
 
 def shards(queries, key_feats, value_feats, filters, grad_out):
@@ -268,12 +301,18 @@
     vmem = pl.BlockSpec(memory_space=pltpu.VMEM)
     dma = pltpu.SemaphoreType.DMA
     like = pltpu.VMEM((tokens, channels), BF16)
-    return pl.pallas_call(
+    anywhere = pl.BlockSpec(memory_space=pl.ANY)
+    parts = channels // PART
+    results = pl.pallas_call(
         functools.partial(kernel, n_ctx, n_mp),
         out_shape=(like, like, like, like, pltpu.VMEM((groups, span), F32)),
-        in_specs=[vmem] * 5,
+        in_specs=[anywhere] * 3 + [vmem, anywhere],
         out_specs=[vmem] * 5,
         scratch_shapes=[
+            pltpu.VMEM((tokens, channels), BF16),
+            pltpu.VMEM((tokens, channels), BF16),
+            pltpu.VMEM((tokens, channels), BF16),
+            pltpu.VMEM((tokens, channels), BF16),
             pltpu.VMEM((tokens, channels), BF16),
             pltpu.VMEM((tokens, channels), BF16),
             pltpu.VMEM((span, channels), BF16),
@@ -289,13 +328,20 @@
             pltpu.VMEM((n_ctx, own, span), F32),
             pltpu.VMEM((8, span), F32),
             pltpu.VMEM((n_mp, 8, span), F32),
-            dma((PARTS,)), dma((PARTS,)), dma((PARTS,)), dma((PARTS,)),
+            dma((parts,)), dma((parts,)), dma((parts,)), dma((parts,)),
             dma((n_ctx,)), dma((n_ctx,)), dma((n_ctx,)), dma((n_ctx,)),
-            dma((n_mp,)), dma((n_mp,)),
+            dma((n_mp,)), dma((n_mp,)), dma((8,)),
         ],
         compiler_params=pltpu.CompilerParams(
             collective_id=0, has_side_effects=True, vmem_limit_bytes=56 * 2**20),
     )(queries, key_feats, value_feats, filters, grad_out)
+    return pl.pallas_call(
+        unload,
+        out_shape=tuple(jax.ShapeDtypeStruct(x.shape, x.dtype) for x in results),
+        in_specs=[vmem] * 5,
+        out_specs=[anywhere] * 5,
+        scratch_shapes=[dma((5,))],
+    )(*results)
 
 
 def solution(mesh):

time: 47.8 us -> 40.5 us (0.85); the launches traced: 47 us -> 40.3 us
  Pallas kernels: 41.8 us -> 35.1 us
    pallas_call x1, Pallas kernels: 41.8 us -> 30.9 us  [shards(): pl.pallas_call(functools.partial(kernel, n_ctx, n_mp), out_shape=(like, l...]
    pallas_call x0 -> x1, Pallas kernels: none -> 4.22 us  [shards(): pl.pallas_call(unload, out_shape=tuple((jax.ShapeDtypeStruct(x.shape, x.d...]
    unnamed x5 -> x10, local copies, waits for them, and re-layouts: 4.51 us -> 4.57 us
where the time goes in v5:
time: 40.5 us; the launch traced here: 40.3 us
  Pallas kernels  35.1 us (87%)
  local copies, waits for them, and re-layouts  4.57 us (11%)
  between operations  0.65 us (2%)
    pallas_call x1, Pallas kernels, shards(): pl.pallas_call(functools.partial(kernel, n_ctx, n_mp), out_shape=(like, l...  30.9 us
    unnamed x10, local copies, waits for them, and re-layouts  4.57 us
    pallas_call x1, Pallas kernels, shards(): pl.pallas_call(unload, out_shape=tuple((jax.ShapeDtypeStruct(x.shape, x.d...  4.22 us

profile of v5, /device:TPU:0, one launch (start us, length us, event | category | flops | bytes accessed | tf_op | source)
XLA Modules:
  0.0 40.3 jit_solution(5904167884297539537)
XLA Ops:
  0.6 30.9 %shard_map.92 = (bf16[256,2048]{1,0:T(8,128)(2,1)S(1)}, bf16[256,2048]{1,0:T(8,128)(2,1)S(1)}, bf16[256,2048]{1,0:T(8,128)(2,1)S(1)}, bf16[256,2048]{1,0:T(8,128)(2,1)S(1)}, f32[128,128]{1,0:T(8,128)S(1)}) custom-call(bf16[256,2048]{1,0:T(8,128)(2,1)} %q_hbm.1, bf16[256,2048]{1,0:T(8,128)(2,1)} %k_hbm.1, bf16[256,2048]{1,0:T(8,128)(2,1)} %v_hbm.1, ...), custom_call_target="tpu_custom_call" | custom-call | tf_op jit(solution)/shard_map/pallas_call | solution.py:306
  31.5 0.0 copy-start
  31.5 1.0 %copy-done = bf16[256,2048]{1,0:T(8,128)(2,1)} copy-done((bf16[256,2048]{1,0:T(8,128)(2,1)}, bf16[256,2048]{1,0:T(8,128)(2,1)S(1)}, u32[]{:S(2)}) %copy-start) | copy-done | bytes 1048600
  32.5 0.0 copy-start.1
  32.5 1.0 %copy-done.1 = bf16[256,2048]{1,0:T(8,128)(2,1)} copy-done((bf16[256,2048]{1,0:T(8,128)(2,1)}, bf16[256,2048]{1,0:T(8,128)(2,1)S(1)}, u32[]{:S(2)}) %copy-start.1) | copy-done | bytes 1048600
  33.5 0.0 copy-start.2
  33.5 1.0 %copy-done.2 = bf16[256,2048]{1,0:T(8,128)(2,1)} copy-done((bf16[256,2048]{1,0:T(8,128)(2,1)}, bf16[256,2048]{1,0:T(8,128)(2,1)S(1)}, u32[]{:S(2)}) %copy-start.2) | copy-done | bytes 1048600
  34.5 0.0 copy-start.3
  34.5 1.0 %copy-done.3 = bf16[256,2048]{1,0:T(8,128)(2,1)} copy-done((bf16[256,2048]{1,0:T(8,128)(2,1)}, bf16[256,2048]{1,0:T(8,128)(2,1)S(1)}, u32[]{:S(2)}) %copy-start.3) | copy-done | bytes 1048600
  35.5 0.0 copy-start.4
  35.5 0.6 %copy-done.4 = f32[128,128]{1,0:T(8,128)} copy-done((f32[128,128]{1,0:T(8,128)}, f32[128,128]{1,0:T(8,128)S(1)}, u32[]{:S(2)}) %copy-start.4) | copy-done | bytes 65560
  36.1 4.2 %shard_map.93 = (bf16[256,2048]{1,0:T(8,128)(2,1)}, bf16[256,2048]{1,0:T(8,128)(2,1)}, bf16[256,2048]{1,0:T(8,128)(2,1)}, bf16[256,2048]{1,0:T(8,128)(2,1)}, f32[128,128]{1,0:T(8,128)}) custom-call(bf16[256,2048]{1,0:T(8,128)(2,1)} %copy-done, bf16[256,2048]{1,0:T(8,128)(2,1)} %copy-done.1, bf16[256,2048]{1,0:T(8,128)(2,1)} %copy-done.2, ...), custom_call_target="tpu_custom_call" | custom-call | tf_op jit(solution)/shard_map/pallas_call | solution.py:338
Async XLA Ops:
  31.5 1.0 %copy-start = (bf16[256,2048]{1,0:T(8,128)(2,1)}, bf16[256,2048]{1,0:T(8,128)(2,1)S(1)}, u32[]{:S(2)}) copy-start(bf16[256,2048]{1,0:T(8,128)(2,1)S(1)} %get-tuple-element.10.a) | copy-start | bytes 3145732
  32.5 1.0 %copy-start.1 = (bf16[256,2048]{1,0:T(8,128)(2,1)}, bf16[256,2048]{1,0:T(8,128)(2,1)S(1)}, u32[]{:S(2)}) copy-start(bf16[256,2048]{1,0:T(8,128)(2,1)S(1)} %get-tuple-element.11.b) | copy-start | bytes 3145732
  33.5 1.0 %copy-start.2 = (bf16[256,2048]{1,0:T(8,128)(2,1)}, bf16[256,2048]{1,0:T(8,128)(2,1)S(1)}, u32[]{:S(2)}) copy-start(bf16[256,2048]{1,0:T(8,128)(2,1)S(1)} %get-tuple-element.12.c) | copy-start | bytes 3145732
  34.5 1.0 %copy-start.3 = (bf16[256,2048]{1,0:T(8,128)(2,1)}, bf16[256,2048]{1,0:T(8,128)(2,1)S(1)}, u32[]{:S(2)}) copy-start(bf16[256,2048]{1,0:T(8,128)(2,1)S(1)} %get-tuple-element.13.d) | copy-start | bytes 3145732
  35.5 0.6 %copy-start.4 = (f32[128,128]{1,0:T(8,128)}, f32[128,128]{1,0:T(8,128)S(1)}, u32[]{:S(2)}) copy-start(f32[128,128]{1,0:T(8,128)S(1)} %get-tuple-element.14.e) | copy-start | bytes 196612

commit v6 on v5

--- a/solution.py
+++ b/solution.py
@@ -57,16 +57,15 @@
         return [pltpu.make_async_copy(a.at[rows, :], b.at[rows, :], load.at[first + i])
                 for i, (a, b, rows) in enumerate(pairs)]
 
-    edges = loads([(g_hbm, g_ref, head), (q_hbm, q_ref, head),
-                   (k_hbm, k_ref, tail), (v_hbm, v_ref, tail)], 0)
-    others = loads([(g_hbm, g_ref, rest_g), (q_hbm, q_ref, rest_g),
-                    (k_hbm, k_ref, rest_p), (v_hbm, v_ref, rest_p)], 4)
+    edges = loads([(g_hbm, g_ref, head), (q_hbm, q_ref, head)], 0)
+    others = loads([(k_hbm, k_ref, tail), (v_hbm, v_ref, tail),
+                    (g_hbm, g_ref, rest_g), (q_hbm, q_ref, rest_g),
+                    (k_hbm, k_ref, rest_p), (v_hbm, v_ref, rest_p)], 2)
     for copy in edges + others:
         copy.start()
     for copy in edges:
         copy.wait()
     gmix[head, :] = times(g_ref[head, :], q_ref[head, :])
-    prod[tail, :] = times(k_ref[tail, :], v_ref[tail, :])
     pl.semaphore_wait(barrier, n_ctx + n_mp - 2)
 
     def g_copy(i):
@@ -89,10 +88,6 @@
         def _():
             g_copy(i).start()
 
-        @pl.when(me < n_ctx - 1)
-        def _():
-            p_copy(i).start()
-
     @pl.when(me == 0)
     def _():
         phalo[...] = jnp.zeros_like(phalo)
@@ -104,7 +99,7 @@
     for copy in others:
         copy.wait()
     gmix[rest_g, :] = times(g_ref[rest_g, :], q_ref[rest_g, :])
-    prod[rest_p, :] = times(k_ref[rest_p, :], v_ref[rest_p, :])
+    prod[...] = times(k_ref[...], v_ref[...])
     taps[...] = f_ref[...].astype(F32)
 
     col = lax.broadcasted_iota(jnp.int32, (span, span), 1)
@@ -126,6 +121,12 @@
         for j in range(per_chunk):
             spread(c * per_chunk + j, taps, toep, upper)
             spread(c * per_chunk + j, flipped, toep_f, col > row)
+
+    @pl.loop(0, parts)
+    def _(i):
+        @pl.when(me < n_ctx - 1)
+        def _():
+            p_copy(i).start()
 
     lane = lax.broadcasted_iota(jnp.int32, (1, blocks * WIDE), 1)
     member = lax.rem(lane, WIDE) // G
@@ -218,7 +219,39 @@
         mix_ref[:, at] = times(ahead, q_ref[:, at])
         gq_ref[:, at] = times(ahead, g_ref[:, at])
 
-    def convs(i):
+    def gather_rows():
+        @pl.loop(1, n_ctx)
+        def _(i):
+            rs_copy(me, ctx_peer(i)).wait_recv()
+
+        reduced[...] = jnp.sum(arrived[...], axis=0)
+
+        @pl.loop(1, n_ctx)
+        def _(i):
+            ag_copy(ctx_peer(i), me).start()
+
+        gathered[me] = reduced[...]
+
+    def share_squares():
+        @pl.loop(1, n_ctx)
+        def _(i):
+            ag_copy(me, ctx_peer(i)).wait_recv()
+
+        raw = gathered[...].reshape(groups, span)
+        squares = jnp.sum(jnp.sum(raw * raw, axis=0, keepdims=True), axis=1, keepdims=True)
+        own_sq[...] = jnp.broadcast_to(squares, own_sq.shape)
+
+        @pl.loop(1, n_mp)
+        def _(i):
+            sq_copy(mp_peer(i), slab).start()
+
+        all_sq[slab] = own_sq[...]
+
+    @pl.loop(0, parts)
+    def _(i):
+        pl.when(i == parts * 3 // 8)(gather_rows)
+        pl.when(i == parts * 6 // 8)(share_squares)
+
         @pl.when(me > 0)
         def _():
             p_copy(i).wait_recv()
@@ -226,40 +259,11 @@
         for c in range(chunks):
             both_convs(i * chunks + c)
 
-    pl.loop(0, parts // 2)(convs)
-
-    @pl.loop(1, n_ctx)
-    def _(i):
-        rs_copy(me, ctx_peer(i)).wait_recv()
-
-    reduced[...] = jnp.sum(arrived[...], axis=0)
-
-    @pl.loop(1, n_ctx)
-    def _(i):
-        ag_copy(ctx_peer(i), me).start()
-
-    gathered[me] = reduced[...]
-
-    pl.loop(parts // 2, parts)(convs)
-
-    @pl.loop(1, n_ctx)
-    def _(i):
-        ag_copy(me, ctx_peer(i)).wait_recv()
+    @pl.loop(1, n_mp)
+    def _(i):
+        sq_copy(slab, mp_peer(i)).wait_recv()
 
     raw = gathered[...].reshape(groups, span)
-    squares = jnp.sum(jnp.sum(raw * raw, axis=0, keepdims=True), axis=1, keepdims=True)
-    own_sq[...] = jnp.broadcast_to(squares, own_sq.shape)
-
-    @pl.loop(1, n_mp)
-    def _(i):
-        sq_copy(mp_peer(i), slab).start()
-
-    all_sq[slab] = own_sq[...]
-
-    @pl.loop(1, n_mp)
-    def _(i):
-        sq_copy(slab, mp_peer(i)).wait_recv()
-
     square_sum = jnp.sum(all_sq[...], axis=0)[0:1, :]
     grad_rms = jnp.sqrt(square_sum / (groups * n_mp * span) + 1e-06)
     gf_ref[...] = raw * jnp.minimum(1.0, 1.0 / grad_rms)
@@ -338,9 +342,10 @@
     return pl.pallas_call(
         unload,
         out_shape=tuple(jax.ShapeDtypeStruct(x.shape, x.dtype) for x in results),
-        in_specs=[vmem] * 5,
+        in_specs=[anywhere] * 5,
         out_specs=[anywhere] * 5,
         scratch_shapes=[dma((5,))],
+        compiler_params=pltpu.CompilerParams(vmem_limit_bytes=8 * 2**20),
     )(*results)
 
 

time: 40.5 us -> 31.9 us (0.79)
  local copies, waits for them, and re-layouts: 4.57 us -> 0 us
  Pallas kernels: 35.1 us -> 31.1 us
    unnamed x10 -> x0, local copies, waits for them, and re-layouts: 4.57 us -> none
    pallas_call x1, Pallas kernels: 4.22 us -> 2.06 us  [shards(): pl.pallas_call(unload, out_shape=tuple((jax.ShapeDtypeStruct(x.shape, x.d...]
    pallas_call x1, Pallas kernels: 30.9 us -> 29.1 us  [shards(): pl.pallas_call(functools.partial(kernel, n_ctx, n_mp), out_shape=(like, l...]
where the time goes in v6:
time: 31.9 us; the launch traced here: 31.8 us
  Pallas kernels  31.1 us (97%)
  between operations  0.64 us (2%)
    pallas_call x1, Pallas kernels, shards(): pl.pallas_call(functools.partial(kernel, n_ctx, n_mp), out_shape=(like, l...  29.1 us
    pallas_call x1, Pallas kernels, shards(): pl.pallas_call(unload, out_shape=tuple((jax.ShapeDtypeStruct(x.shape, x.d...  2.06 us

profile of v6, /device:TPU:0, one launch (start us, length us, event | category | flops | bytes accessed | tf_op | source)
XLA Modules:
  0.0 31.8 jit_solution(5377551220159600974)
XLA Ops:
  0.6 29.1 %shard_map.92 = (bf16[256,2048]{1,0:T(8,128)(2,1)S(1)}, bf16[256,2048]{1,0:T(8,128)(2,1)S(1)}, bf16[256,2048]{1,0:T(8,128)(2,1)S(1)}, bf16[256,2048]{1,0:T(8,128)(2,1)S(1)}, f32[128,128]{1,0:T(8,128)S(1)}) custom-call(bf16[256,2048]{1,0:T(8,128)(2,1)} %q_hbm.1, bf16[256,2048]{1,0:T(8,128)(2,1)} %k_hbm.1, bf16[256,2048]{1,0:T(8,128)(2,1)} %v_hbm.1, ...), custom_call_target="tpu_custom_call" | custom-call | tf_op jit(solution)/shard_map/pallas_call | solution.py:310
  29.7 2.1 %shard_map.93 = (bf16[256,2048]{1,0:T(8,128)(2,1)}, bf16[256,2048]{1,0:T(8,128)(2,1)}, bf16[256,2048]{1,0:T(8,128)(2,1)}, bf16[256,2048]{1,0:T(8,128)(2,1)}, f32[128,128]{1,0:T(8,128)}) custom-call(bf16[256,2048]{1,0:T(8,128)(2,1)S(1)} %get-tuple-element.10.a, bf16[256,2048]{1,0:T(8,128)(2,1)S(1)} %get-tuple-element.11.b, ...), custom_call_target="tpu_custom_call" | custom-call | tf_op jit(solution)/shard_map/pallas_call | solution.py:342

commit v7 on v6

--- a/solution.py
+++ b/solution.py
@@ -65,7 +65,6 @@
         copy.start()
     for copy in edges:
         copy.wait()
-    gmix[head, :] = times(g_ref[head, :], q_ref[head, :])
     pl.semaphore_wait(barrier, n_ctx + n_mp - 2)
 
     def g_copy(i):
@@ -84,6 +83,9 @@
 
     @pl.loop(0, parts)
     def _(i):
+        cols = pl.ds(pl.multiple_of(i * PART, PART), PART)
+        gmix[head, cols] = times(g_ref[head, cols], q_ref[head, cols])
+
         @pl.when(me > 0)
         def _():
             g_copy(i).start()
@@ -98,8 +100,13 @@
 
     for copy in others:
         copy.wait()
-    gmix[rest_g, :] = times(g_ref[rest_g, :], q_ref[rest_g, :])
-    prod[...] = times(k_ref[...], v_ref[...])
+
+    @pl.loop(0, parts)
+    def _(i):
+        cols = pl.ds(pl.multiple_of(i * PART, PART), PART)
+        gmix[rest_g, cols] = times(g_ref[rest_g, cols], q_ref[rest_g, cols])
+        prod[:, cols] = times(k_ref[:, cols], v_ref[:, cols])
+
     taps[...] = f_ref[...].astype(F32)
 
     col = lax.broadcasted_iota(jnp.int32, (span, span), 1)
@@ -116,17 +123,10 @@
         out[i, :, 0:span] = jnp.where(mask, turned, zero).astype(BF16)
         out[i, :, span:] = jnp.where(mask, zero, turned).astype(BF16)
 
-    @pl.loop(0, groups // per_chunk)
-    def _(c):
+    def build(c):
         for j in range(per_chunk):
             spread(c * per_chunk + j, taps, toep, upper)
             spread(c * per_chunk + j, flipped, toep_f, col > row)
-
-    @pl.loop(0, parts)
-    def _(i):
-        @pl.when(me < n_ctx - 1)
-        def _():
-            p_copy(i).start()
 
     lane = lax.broadcasted_iota(jnp.int32, (1, blocks * WIDE), 1)
     member = lax.rem(lane, WIDE) // G
@@ -157,12 +157,13 @@
 
     def correlate(c):
         at = pl.ds(pl.multiple_of(c * WIDE, WIDE), WIDE)
-        wins = g_windows(at).T
+        wins = g_windows(at)
         left = jnp.concatenate(
             [prod[n * span:(n + 1) * span, at] for n in range(blocks)], axis=1)
         mine = jnp.concatenate(
             [jnp.where(member == j, left, jnp.zeros_like(left)) for j in range(per_chunk)], axis=0)
-        every = jnp.dot(mine, wins, preferred_element_type=F32)
+        every = lax.dot_general(mine, wins, (((1,), (1,)), ((), ())),
+                                preferred_element_type=F32)
         for j in range(per_chunk):
             both = every[j * span:(j + 1) * span]
             turn = jnp.where(upper, both[:, :span], both[:, span:])
@@ -178,7 +179,12 @@
         def _():
             g_copy(i).wait_recv()
 
+        @pl.when(me < n_ctx - 1)
+        def _():
+            p_copy(i).start()
+
         for c in range(chunks):
+            build(i * chunks + c)
             correlate(i * chunks + c)
 
     total = folded[pl.ds(0, groups, stride=8), :]

time: 31.9 us -> 31.3 us (0.981)
  Pallas kernels: 31.1 us -> 30.5 us
    pallas_call x1, Pallas kernels: 29.1 us -> 28.4 us  [shards(): pl.pallas_call(functools.partial(kernel, n_ctx, n_mp), out_shape=(like, l...]
where the time goes in v7:
time: 31.3 us; the launch traced here: 31.1 us
  Pallas kernels  30.5 us (97%)
  between operations  0.64 us (2%)
    pallas_call x1, Pallas kernels, shards(): pl.pallas_call(functools.partial(kernel, n_ctx, n_mp), out_shape=(like, l...  28.4 us
    pallas_call x1, Pallas kernels, shards(): pl.pallas_call(unload, out_shape=tuple((jax.ShapeDtypeStruct(x.shape, x.d...  2.06 us

profile of v7, /device:TPU:0, one launch (start us, length us, event | category | flops | bytes accessed | tf_op | source)
XLA Modules:
  0.0 31.1 jit_solution(10491250737329865366)
XLA Ops:
  0.6 28.4 %shard_map.92 = (bf16[256,2048]{1,0:T(8,128)(2,1)S(1)}, bf16[256,2048]{1,0:T(8,128)(2,1)S(1)}, bf16[256,2048]{1,0:T(8,128)(2,1)S(1)}, bf16[256,2048]{1,0:T(8,128)(2,1)S(1)}, f32[128,128]{1,0:T(8,128)S(1)}) custom-call(bf16[256,2048]{1,0:T(8,128)(2,1)} %q_hbm.1, bf16[256,2048]{1,0:T(8,128)(2,1)} %k_hbm.1, bf16[256,2048]{1,0:T(8,128)(2,1)} %v_hbm.1, ...), custom_call_target="tpu_custom_call" | custom-call | tf_op jit(solution)/shard_map/pallas_call | solution.py:316
  29.1 2.1 %shard_map.93 = (bf16[256,2048]{1,0:T(8,128)(2,1)}, bf16[256,2048]{1,0:T(8,128)(2,1)}, bf16[256,2048]{1,0:T(8,128)(2,1)}, bf16[256,2048]{1,0:T(8,128)(2,1)}, f32[128,128]{1,0:T(8,128)}) custom-call(bf16[256,2048]{1,0:T(8,128)(2,1)S(1)} %get-tuple-element.10.a, bf16[256,2048]{1,0:T(8,128)(2,1)S(1)} %get-tuple-element.11.b, ...), custom_call_target="tpu_custom_call" | custom-call | tf_op jit(solution)/shard_map/pallas_call | solution.py:348

commit v8 on v7

--- a/solution.py
+++ b/solution.py
@@ -12,7 +12,7 @@
 F32 = jnp.float32
 BF16 = jnp.bfloat16
 WIDE = 128
-PART = 256
+PART = 512
 
 
 def times(a, b):

time: 31.3 us -> 34.5 us (1.10)
  Pallas kernels: 30.5 us -> 33.7 us
    pallas_call x1, Pallas kernels: 28.4 us -> 31.7 us  [shards(): pl.pallas_call(functools.partial(kernel, n_ctx, n_mp), out_shape=(like, l...]
where the time goes in v8:
time: 34.5 us; the launch traced here: 34.4 us
  Pallas kernels  33.7 us (98%)
  between operations  0.64 us (2%)
    pallas_call x1, Pallas kernels, shards(): pl.pallas_call(functools.partial(kernel, n_ctx, n_mp), out_shape=(like, l...  31.7 us
    pallas_call x1, Pallas kernels, shards(): pl.pallas_call(unload, out_shape=tuple((jax.ShapeDtypeStruct(x.shape, x.d...  2.06 us

profile of v8, /device:TPU:0, one launch (start us, length us, event | category | flops | bytes accessed | tf_op | source)
XLA Modules:
  0.0 34.4 jit_solution(12340489756436827258)
XLA Ops:
  0.6 31.7 %shard_map.92 = (bf16[256,2048]{1,0:T(8,128)(2,1)S(1)}, bf16[256,2048]{1,0:T(8,128)(2,1)S(1)}, bf16[256,2048]{1,0:T(8,128)(2,1)S(1)}, bf16[256,2048]{1,0:T(8,128)(2,1)S(1)}, f32[128,128]{1,0:T(8,128)S(1)}) custom-call(bf16[256,2048]{1,0:T(8,128)(2,1)} %q_hbm.1, bf16[256,2048]{1,0:T(8,128)(2,1)} %k_hbm.1, bf16[256,2048]{1,0:T(8,128)(2,1)} %v_hbm.1, ...), custom_call_target="tpu_custom_call" | custom-call | tf_op jit(solution)/shard_map/pallas_call | solution.py:316
  32.3 2.1 %shard_map.93 = (bf16[256,2048]{1,0:T(8,128)(2,1)}, bf16[256,2048]{1,0:T(8,128)(2,1)}, bf16[256,2048]{1,0:T(8,128)(2,1)}, bf16[256,2048]{1,0:T(8,128)(2,1)}, f32[128,128]{1,0:T(8,128)}) custom-call(bf16[256,2048]{1,0:T(8,128)(2,1)S(1)} %get-tuple-element.10.a, bf16[256,2048]{1,0:T(8,128)(2,1)S(1)} %get-tuple-element.11.b, ...), custom_call_target="tpu_custom_call" | custom-call | tf_op jit(solution)/shard_map/pallas_call | solution.py:348
